TPU v7x, 256 devices: a whole 4x4x8 slice. The times are simulated.
256 devices in a mesh: blk: 64 (over y_lo, x, z), uly: 4 (over y_hi, core).
Axes of the slice: x: 4, y: 4 (y_hi: 2, y_lo: 2; y = y_hi * 2 + y_lo), z: 8, core: 2. Of those that a mesh axis runs over, the one named last changes fastest.
Arguments:
- queries: bfloat16 [32768, 3072], P(('blk', 'uly')), may hold values from -40 to 40
- keys: bfloat16 [32768, 3072], P(('blk', 'uly')), may hold values from -8 to 8
- values: bfloat16 [32768, 3072], P(('blk', 'uly')), may hold values from -6 to 6
- tile_order: int32 [256], replicated, may hold values from 0 to 255, as said below
- tile_mask: int32 [256, 20], replicated, may hold values from 0 to 1, as said below
Outputs:
- attended: bfloat16 [32768, 3072], P(('blk', 'uly'))
Inputs may be any that keep to these rules, and one draw needn't show every extreme that they name: `tile_order`: entries 4 * f to 4 * f + 3 are a permutation of the tile numbers 4 * f to 4 * f + 3: every slot holds a tile of its own frame. tile_mask[a, (e + 2) * 4 + b] is 1 where tile a may attend to tile 4 * (a // 4 + e) + b; it is 0 where a // 4 + e is not a frame; tile_mask[a, 8 + a % 4] is 1.
All inputs are finite; a program needn't handle non-finite values.
Results may differ from a plain program's by a relative error of at most 0.0055.
Values may be sent and summed in bfloat16 or wider, within the bound.
No kernel may reach another device: no remote copies, remote signals or barrier semaphores. Data moves between devices by JAX's collectives and lax.ppermute only.
A program may use at most 64 MiB of HBM per device.

v0:
```python
import math
import jax
import jax.numpy as jnp
from jax import lax
from jax.sharding import PartitionSpec as P

HEAD = 128
TPS = 4
REACH = 2


def passed_along(block, axis, distance):
    devices = range(lax.axis_size(axis))
    route = [((i - distance) % len(devices), i) for i in devices]
    return lax.ppermute(block, axis, route)


def select_matrix(indices, count):
    return (indices[:, None] == jnp.arange(count, dtype=jnp.int32)[None, :]).astype(jnp.float32)


def per_device(queries, keys, values, tile_order, tile_mask):
    head_queries, head_keys, head_values = (
        lax.all_to_all(queries, "uly", split_axis=1, concat_axis=0, tiled=True),
        lax.all_to_all(keys, "uly", split_axis=1, concat_axis=0, tiled=True),
        lax.all_to_all(values, "uly", split_axis=1, concat_axis=0, tiled=True),
    )
    block_rows = head_queries.shape[0]
    local_heads = head_queries.shape[1] // HEAD
    tile_rows = block_rows // TPS
    position = lax.axis_index("blk")
    frame_count = lax.axis_size("blk")
    scale = 1.0 / math.sqrt(HEAD)
    query_heads = head_queries.reshape(block_rows, local_heads, HEAD)
    own_order = lax.dynamic_slice_in_dim(tile_order, position * TPS, TPS) - position * TPS
    own_rows = lax.dynamic_slice_in_dim(tile_mask, position * TPS, TPS, 0).astype(jnp.float32)
    slot_rows = jnp.dot(
        select_matrix(own_order, TPS),
        own_rows,
        precision=lax.Precision.HIGHEST,
        preferred_element_type=jnp.float32,
    )

    def absorb(state, stacked, offset):
        other_frame = position + offset
        inside = ((other_frame >= 0) & (other_frame < frame_count)).astype(jnp.float32)
        clipped = jnp.clip(other_frame, 0, frame_count - 1)
        other_order = lax.dynamic_slice_in_dim(tile_order, clipped * TPS, TPS) - clipped * TPS
        columns = slot_rows[:, (offset + REACH) * TPS : (offset + REACH + 1) * TPS]
        tile_allowed = (
            jnp.dot(
                columns,
                select_matrix(other_order, TPS).T,
                precision=lax.Precision.HIGHEST,
                preferred_element_type=jnp.float32,
            )
            * inside
        )
        active = jnp.any(tile_allowed > 0.5)

        def update(carried):
            top_score, total, accum = carried
            allowed = jnp.repeat(
                jnp.repeat(tile_allowed > 0.5, tile_rows, axis=0), tile_rows, axis=1
            )
            key_heads = stacked[0].reshape(block_rows, local_heads, HEAD)
            value_heads = stacked[1].reshape(block_rows, local_heads, HEAD)
            scores = (
                jnp.einsum(
                    "qhd,khd->qhk", query_heads, key_heads, preferred_element_type=jnp.float32
                )
                * scale
            )
            masked = jnp.where(allowed[:, None, :], scores, -1e30)
            new_top = jnp.maximum(top_score, jnp.max(masked, axis=2))
            weights = jnp.where(allowed[:, None, :], jnp.exp(masked - new_top[:, :, None]), 0.0)
            factor = jnp.exp(top_score - new_top)
            new_total = total * factor + jnp.sum(weights, axis=2)
            new_accum = accum * factor[:, :, None] + jnp.einsum(
                "qhk,khd->qhd",
                weights.astype(jnp.bfloat16),
                value_heads,
                preferred_element_type=jnp.float32,
            )
            return (new_top, new_total, new_accum)

        def unchanged(carried):
            return carried

        return lax.cond(active, update, unchanged, state)

    state = (
        jnp.full((block_rows, local_heads), -1e30, jnp.float32),
        jnp.zeros((block_rows, local_heads), jnp.float32),
        jnp.zeros((block_rows, local_heads, HEAD), jnp.float32),
    )
    own_pair = jnp.stack([head_keys, head_values])
    arriving = passed_along(own_pair, "blk", -REACH)
    state = absorb(state, arriving, REACH)
    for step_index in range(2 * REACH):
        arriving = passed_along(arriving, "blk", 1)
        state = absorb(state, arriving, REACH - 1 - step_index)
    top_score, total, accum = state
    outputs = (
        (accum / total[:, :, None]).astype(jnp.bfloat16).reshape(block_rows, local_heads * HEAD)
    )
    return lax.all_to_all(outputs, "uly", split_axis=0, concat_axis=1, tiled=True)


def solution(mesh):
    return jax.shard_map(
        per_device,
        mesh=mesh,
        in_specs=(
            P(("blk", "uly"), None),
            P(("blk", "uly"), None),
            P(("blk", "uly"), None),
            P(),
            P(),
        ),
        out_specs=P(("blk", "uly"), None),
        check_vma=False,
    )
```

profile of v0, /device:TPU:8, one launch (start us, length us, event | category | flops | bytes accessed | tf_op | source)
XLA Modules:
  0.0 353.7 jit_solution(8033766370934859093)
XLA Ops:
  0.0 2.4 copy.125
  2.4 3.6 %all-to-all-start = ((bf16[128,4,768]{0,2,1:T(8,128)(2,1)}), bf16[128,4,768]{0,2,1:T(8,128)(2,1)S(1)}, u32[]{:S(2)}, u32[]{:S(2)}) async-start(bf16[128,4,768]{0,2,1:T(8,128)(2,1)} %bitcast.25), calls=%async_computation | async-start | bytes 1572864 | tf_op jit(solution)/shard_map/all_to_all | solution.py:25
  5.9 2.3 copy.127
  8.2 10.9 %all-to-all-done = bf16[128,4,768]{0,2,1:T(8,128)(2,1)S(1)} async-done(((bf16[128,4,768]{0,2,1:T(8,128)(2,1)}), bf16[128,4,768]{0,2,1:T(8,128)(2,1)S(1)}, u32[]{:S(2)}, u32[]{:S(2)}) %all-to-all-start) | async-done | bytes 786464 | tf_op jit(solution)/shard_map/all_to_all | solution.py:25
  19.1 3.5 all-to-all-start.1
  22.9 12.8 %all-to-all-done.1 = bf16[128,4,768]{0,2,1:T(8,128)(2,1)S(1)} async-done(((bf16[128,4,768]{0,2,1:T(8,128)(2,1)}), bf16[128,4,768]{0,2,1:T(8,128)(2,1)S(1)}, u32[]{:S(2)}, u32[]{:S(2)}) %all-to-all-start.1) | async-done | bytes 786464 | tf_op jit(solution)/shard_map/all_to_all | solution.py:26
  36.2 9.4 %collective-permute-start = (bf16[2,512,768]{2,1,0:T(8,128)(2,1)S(1)}, bf16[2,512,768]{2,1,0:T(8,128)(2,1)S(1)}, u32[]{:S(2)}, u32[]{:S(2)}) collective-permute-start(bf16[2,512,768]{2,1,0:T(8,128)(2,1)S(1)} %pad_maximum_fusion), channel_id=1, source_target_pairs={{8,0},{12,4},{16,8},{20,12},{24,16},{28,20},{32,24},{36,28},{40,32... | collective-permute-start | bytes 4718600 | tf_op jit(solution)/shard_map/ppermute | solution.py:15
  45.5 67.2 %collective-permute-done = bf16[2,512,768]{2,1,0:T(8,128)(2,1)S(1)} collective-permute-done((bf16[2,512,768]{2,1,0:T(8,128)(2,1)S(1)}, bf16[2,512,768]{2,1,0:T(8,128)(2,1)S(1)}, u32[]{:S(2)}, u32[]{:S(2)}) %collective-permute-start) | collective-permute-done | bytes 1572896 | tf_op jit(solution)/shard_map/ppermute | solution.py:15
  112.7 1.1 copy-done.2
  113.8 38.9 %collective-permute-done.1 = bf16[2,512,768]{2,1,0:T(8,128)(2,1)S(1)} collective-permute-done((bf16[2,512,768]{2,1,0:T(8,128)(2,1)S(1)}, bf16[2,512,768]{2,1,0:T(8,128)(2,1)S(1)}, u32[]{:S(2)}, u32[]{:S(2)}) %collective-permute-start.1) | collective-permute-done | bytes 1572896 | tf_op jit(solution)/shard_map/ppermute | solution.py:15
  152.7 39.1 %collective-permute-done.2 = bf16[2,512,768]{2,1,0:T(8,128)(2,1)S(1)} collective-permute-done((bf16[2,512,768]{2,1,0:T(8,128)(2,1)S(1)}, bf16[2,512,768]{2,1,0:T(8,128)(2,1)S(1)}, u32[]{:S(2)}, u32[]{:S(2)}) %collective-permute-start.2) | collective-permute-done | bytes 1572896 | tf_op jit(solution)/shard_map/ppermute | solution.py:15
  191.8 1.1 copy-done
  193.0 38.3 %collective-permute-done.3 = bf16[2,512,768]{2,1,0:T(8,128)(2,1)} collective-permute-done((bf16[2,512,768]{2,1,0:T(8,128)(2,1)S(1)}, bf16[2,512,768]{2,1,0:T(8,128)(2,1)}, u32[]{:S(2)}, u32[]{:S(2)}) %collective-permute-start.3) | collective-permute-done | bytes 1572896 | tf_op jit(solution)/shard_map/ppermute | solution.py:15
  231.3 1.2 copy.129
  232.4 3.5 all-to-all-start.2
  236.3 0.9 compare_reduce_fusion
  237.8 0.9 compare_reduce_fusion.1
  239.3 0.9 compare_reduce_fusion.2
  240.8 0.9 compare_reduce_fusion.3
  242.3 0.8 compare_reduce_fusion.4
  243.7 32.0 %all-to-all-done.2 = bf16[128,4,768]{0,2,1:T(8,128)(2,1)S(1)} async-done(((bf16[128,4,768]{0,2,1:T(8,128)(2,1)}), bf16[128,4,768]{0,2,1:T(8,128)(2,1)S(1)}, u32[]{:S(2)}, u32[]{:S(2)}) %all-to-all-start.2) | async-done | bytes 786464 | tf_op jit(solution)/shard_map/all_to_all | solution.py:24
  275.7 0.6 copy.130
  276.6 10.7 %conditional.5 = (f32[512,6]{0,1:T(8,128)}, f32[512,6]{0,1:T(8,128)S(1)}, f32[512,6,128]{2,0,1:T(8,128)S(1)}) conditional(s32[]{:T(128)} %convert_element_type.67, () %tuple.38, (f32[4,4]{1,0:T(4,128)S(1)}, bf16[2,512,768]{2,1,0:T(8,128)(2,1)}, bf16[512,6,128]{0,2,1:T(8,128)(2,1)S(1)}) %tuple.115), branch_computations={%region_5.6_spmd, %region_6.0_spmd} | conditional | flops 826159104 | bytes 30290168 | solution.py:90
  277.4 1.7 copy.132
  279.2 1.3 fusion
  280.6 0.6 exponential_multiply_fusion
  281.2 2.2 fusion.2
  283.4 0.7 fusion.11
  284.2 3.2 bitcast_add_fusion
  287.4 12.0 %conditional.6 = ((f32[512,6]{0,1:T(8,128)}, f32[512,6]{0,1:T(8,128)S(1)}, f32[512,6,128]{2,0,1:T(8,128)S(1)})) conditional(s32[]{:T(128)} %convert_element_type.65, (f32[512,6]{0,1:T(8,128)}, f32[512,6]{0,1:T(8,128)S(1)}, f32[512,6,128]{2,0,1:T(8,128)S(1)}) %conditional.5, (f32[4,4]{1,0:T(4,128)S(1)}, bf16[2,512,768]{2,1,0:T(8,128)(2,1)}, ...), branch_computations={%region_9.10_spmd, %region_10.0_spmd} | conditional | flops 826546176 | bytes 31924480 | solution.py:90
  287.7 2.6 copy.135
  290.3 1.5 fusion.72
  291.7 1.3 fusion.12
  293.1 0.7 max.19
  293.8 1.5 fusion.14
  295.3 0.7 multiply_add_fusion
  296.1 2.8 bitcast_add_fusion.1
  298.8 0.6 copy.193
  299.4 12.2 %conditional.7 = ((f32[512,6]{0,1:T(8,128)}, f32[512,6]{0,1:T(8,128)S(1)}, f32[512,6,128]{2,0,1:T(8,128)S(1)})) conditional(s32[]{:T(128)} %convert_element_type.63, (f32[512,6]{0,1:T(8,128)}, f32[512,6]{0,1:T(8,128)S(1)}, f32[512,6,128]{2,0,1:T(8,128)S(1)}) %get-tuple-element.345, (f32[4,4]{1,0:T(4,128)S(1)}, bf16[2,512,768]{2,1,0:T(8,128)(2,1)}, ...), branch_computations={%region_13.14_spmd, %region_14.17_spmd} | conditional | flops 826546176 | bytes 31924480 | solution.py:90
  299.9 2.6 copy.138
  302.5 1.5 fusion.73
  304.0 1.3 fusion.23
  305.3 0.7 max.20
  306.0 1.5 fusion.25
  307.5 0.7 multiply_add_fusion.1
  308.3 2.8 bitcast_add_fusion.2
  311.7 12.1 %conditional.8 = ((f32[512,6]{0,1:T(8,128)}, f32[512,6]{0,1:T(8,128)S(1)}, f32[512,6,128]{2,0,1:T(8,128)S(1)})) conditional(s32[]{:T(128)} %convert_element_type.61, (f32[512,6]{0,1:T(8,128)}, f32[512,6]{0,1:T(8,128)S(1)}, f32[512,6,128]{2,0,1:T(8,128)S(1)}) %get-tuple-element.346, (f32[4,4]{1,0:T(4,128)S(1)}, bf16[2,512,768]{2,1,0:T(8,128)(2,1)}, ...), branch_computations={%region_17.18_spmd, %region_18.21_spmd} | conditional | flops 826546176 | bytes 31924480 | solution.py:90
  311.9 2.6 copy.141
  314.5 1.5 fusion.74
  316.0 1.3 fusion.34
  317.3 0.7 max.21
  318.1 1.5 fusion.36
  319.6 0.7 multiply_add_fusion.2
  320.3 2.8 bitcast_add_fusion.3
  323.7 11.6 %conditional.9 = ((f32[512,6]{0,1:T(8,128)S(1)}, f32[512,6,128]{2,0,1:T(8,128)S(1)})) conditional(s32[]{:T(128)} %convert_element_type.59, (f32[512,6]{0,1:T(8,128)S(1)}, f32[512,6,128]{2,0,1:T(8,128)S(1)}) %tuple.43, (f32[4,4]{1,0:T(4,128)S(1)}, bf16[2,512,768]{2,1,0:T(8,128)(2,1)}, bf16[512,6,128]{0,2,1:T(8,128)(2,1)S(1)}, f32[512,6]{0,1:T(8,128)}, ...), branch_computations={%region_21.22_spmd, %region_22.25_spmd} | conditional | flops 826546176 | bytes 31899896 | solution.py:90
  324.2 2.6 copy.144
  326.8 1.5 fusion.75
  328.3 1.3 fusion.45
  329.6 0.7 max.22
  330.3 1.5 fusion.47
  331.8 0.7 multiply_add_fusion.3
  332.6 2.8 bitcast_add_fusion.4
  336.4 15.9 %all_to_all.67 = bf16[4,128,768]{1,2,0:T(8,128)(2,1)S(1)} all-to-all(bf16[4,128,768]{1,2,0:T(8,128)(2,1)S(1)} %copy.147), channel_id=1, replica_groups=mesh['blk'=64,'uly'=4] {'uly'}, dimensions={0} | all-to-all | bytes 1572864 | tf_op jit(solution)/shard_map/all_to_all | solution.py:107
  352.3 1.2 copy.148
  (53 shorter events, 5.0 us)
Async XLA Ops:
  0.0 231.3 %copy-start.3 = (bf16[128,3072]{1,0:T(8,128)(2,1)S(1)}, bf16[128,3072]{1,0:T(8,128)(2,1)}, u32[]{:S(2)}) copy-start(bf16[128,3072]{1,0:T(8,128)(2,1)} %param.15) | copy-start | bytes 2359300
  2.4 16.7 %all-to-all-start = ((bf16[128,4,768]{0,2,1:T(8,128)(2,1)}), bf16[128,4,768]{0,2,1:T(8,128)(2,1)S(1)}, u32[]{:S(2)}, u32[]{:S(2)}) async-start(bf16[128,4,768]{0,2,1:T(8,128)(2,1)} %bitcast.25), calls=%async_computation | async-start | bytes 1572864 | tf_op jit(solution)/shard_map/all_to_all | solution.py:25
  5.9 230.0 %copy-start.4 = (s32[256]{0:T(256)S(1)}, s32[256]{0:T(256)}, u32[]{:S(2)}) copy-start(s32[256]{0:T(256)} %param.18) | copy-start | bytes 3076
  5.9 230.1 %copy-start.5 = (s32[256,20]{0,1:T(8,128)S(1)}, s32[256,20]{0,1:T(8,128)}, u32[]{:S(2)}) copy-start(s32[256,20]{0,1:T(8,128)} %param.19) | copy-start | bytes 61444
  19.1 16.6 %all-to-all-start.1 = ((bf16[128,4,768]{0,2,1:T(8,128)(2,1)}), bf16[128,4,768]{0,2,1:T(8,128)(2,1)S(1)}, u32[]{:S(2)}, u32[]{:S(2)}) async-start(bf16[128,4,768]{0,2,1:T(8,128)(2,1)} %bitcast.28), calls=%async_computation.1 | async-start | bytes 1572864 | tf_op jit(solution)/shard_map/all_to_all | solution.py:26
  36.2 76.5 %collective-permute-start = (bf16[2,512,768]{2,1,0:T(8,128)(2,1)S(1)}, bf16[2,512,768]{2,1,0:T(8,128)(2,1)S(1)}, u32[]{:S(2)}, u32[]{:S(2)}) collective-permute-start(bf16[2,512,768]{2,1,0:T(8,128)(2,1)S(1)} %pad_maximum_fusion), channel_id=1, source_target_pairs={{8,0},{12,4},{16,8},{20,12},{24,16},{28,20},{32,24},{36,28},{40,32... | collective-permute-start | bytes 4718600 | tf_op jit(solution)/shard_map/ppermute | solution.py:15
  112.7 1.1 copy-start.2
  112.7 40.0 %collective-permute-start.1 = (bf16[2,512,768]{2,1,0:T(8,128)(2,1)S(1)}, bf16[2,512,768]{2,1,0:T(8,128)(2,1)S(1)}, u32[]{:S(2)}, u32[]{:S(2)}) collective-permute-start(bf16[2,512,768]{2,1,0:T(8,128)(2,1)S(1)} %collective-permute-done), channel_id=1, source_target_pairs={{252,0},{0,4},{4,8},{8,12},{12,16},{16,20},{20,24},{24,28},{28,32}... | collective-permute-start | bytes 4718600 | tf_op jit(solution)/shard_map/ppermute | solution.py:15
  152.7 78.6 %copy-start.1 = (bf16[2,512,768]{2,1,0:T(8,128)(2,1)}, bf16[2,512,768]{2,1,0:T(8,128)(2,1)S(1)}, u32[]{:S(2)}) copy-start(bf16[2,512,768]{2,1,0:T(8,128)(2,1)S(1)} %collective-permute-done.1) | copy-start | bytes 4718596
  152.7 39.1 %collective-permute-start.2 = (bf16[2,512,768]{2,1,0:T(8,128)(2,1)S(1)}, bf16[2,512,768]{2,1,0:T(8,128)(2,1)S(1)}, u32[]{:S(2)}, u32[]{:S(2)}) collective-permute-start(bf16[2,512,768]{2,1,0:T(8,128)(2,1)S(1)} %collective-permute-done.1), channel_id=1, source_target_pairs={{252,0},{0,4},{4,8},{8,12},{12,16},{16,20},{20,24},{24,28},{28,32}... | collective-permute-start | bytes 4718600 | tf_op jit(solution)/shard_map/ppermute | solution.py:15
  191.8 1.1 copy-start
  193.0 38.3 %collective-permute-start.3 = (bf16[2,512,768]{2,1,0:T(8,128)(2,1)S(1)}, bf16[2,512,768]{2,1,0:T(8,128)(2,1)}, u32[]{:S(2)}, u32[]{:S(2)}) collective-permute-start(bf16[2,512,768]{2,1,0:T(8,128)(2,1)S(1)} %collective-permute-done.2), channel_id=1, source_target_pairs={{252,0},{0,4},{4,8},{8,12},{12,16},{16,20},{20,24},{24,28},{28,32}... | collective-permute-start | bytes 4718600 | tf_op jit(solution)/shard_map/ppermute | solution.py:15
  231.3 92.4 %collective-permute-start.4 = (bf16[2,512,768]{2,1,0:T(8,128)(2,1)}, bf16[2,512,768]{2,1,0:T(8,128)(2,1)}, u32[]{:S(2)}, u32[]{:S(2)}) collective-permute-start(bf16[2,512,768]{2,1,0:T(8,128)(2,1)} %collective-permute-done.3), channel_id=1, source_target_pairs={{252,0},{0,4},{4,8},{8,12},{12,16},{16,20},{20,24},{24,28},{28,32}... | collective-permute-start | bytes 4718600 | tf_op jit(solution)/shard_map/ppermute | solution.py:15
  232.4 43.3 %all-to-all-start.2 = ((bf16[128,4,768]{0,2,1:T(8,128)(2,1)}), bf16[128,4,768]{0,2,1:T(8,128)(2,1)S(1)}, u32[]{:S(2)}, u32[]{:S(2)}) async-start(bf16[128,4,768]{0,2,1:T(8,128)(2,1)} %bitcast.31), calls=%async_computation.2 | async-start | bytes 1572864 | tf_op jit(solution)/shard_map/all_to_all | solution.py:24
where the time goes:
time: 360 us; the launch traced here: 354 us
  waiting for transfers between devices  239 us (66%)
  local copies, waits for them, and re-layouts  32.5 us (9%)
  matrix products  25.4 us (7%)
  starting transfers between devices  19.9 us (6%)
  other arithmetic  16.3 us (5%)
  blocking collectives  15.9 us (4%)
    ppermute x5, waiting for transfers between devices, passed_along(): return lax.ppermute(block, axis, route)  183 us
    all_to_all x1, waiting for transfers between devices, per_device(): lax.all_to_all(queries, 'uly', split_axis=1, concat_axis=0, tiled=True)  32 us
    all_to_all x1, blocking collectives, per_device(): lax.all_to_all(outputs, 'uly', split_axis=0, concat_axis=1, tiled=True)  15.9 us
    dot_general x5, matrix products, update(): jnp.einsum('qhk,khd->qhd', weights.astype(jnp.bfloat16), value_heads, pre...  14.3 us
    all_to_all x1, waiting for transfers between devices, per_device(): lax.all_to_all(values, 'uly', split_axis=1, concat_axis=0, tiled=True)  12.8 us
    another operation x10, local copies, waits for them, and re-layouts  12.6 us
    all_to_all x1, waiting for transfers between devices, per_device(): lax.all_to_all(keys, 'uly', split_axis=1, concat_axis=0, tiled=True)  10.9 us
    ppermute x5, starting transfers between devices, passed_along(): return lax.ppermute(block, axis, route)  9.37 us
  transfers between devices with their start and end apart: 8, of which 7 were waited for; matrix products, arithmetic and copies ran while one was open for 16% of the time, Pallas kernels for 0%

commit v1 on v0

--- a/solution.py
+++ b/solution.py
@@ -21,7 +21,12 @@
 
 def per_device(queries, keys, values, tile_order, tile_mask):
     head_queries, head_keys, head_values = (
-        lax.all_to_all(queries, "uly", split_axis=1, concat_axis=0, tiled=True),
+        jnp.concatenate(
+            lax.all_to_all(
+                jnp.stack(jnp.split(queries, lax.axis_size("uly"), axis=1)), "uly", 0, 0
+            ),
+            axis=0,
+        ),
         lax.all_to_all(keys, "uly", split_axis=1, concat_axis=0, tiled=True),
         lax.all_to_all(values, "uly", split_axis=1, concat_axis=0, tiled=True),
     )

time: 360 us -> 360 us (level)
    unnamed x15 -> x14, local copies, waits for them, and re-layouts: 8.12 us -> 5.84 us
    another operation x10 -> x12, local copies, waits for them, and re-layouts: 12.6 us -> 12.9 us
where the time goes in v1:
time: 360 us; the launch traced here: 354 us
  waiting for transfers between devices  240 us (67%)
  local copies, waits for them, and re-layouts  30.3 us (8%)
  matrix products  25.7 us (7%)
  starting transfers between devices  20.1 us (6%)
  other arithmetic  17.2 us (5%)
  blocking collectives  15.9 us (4%)
  between operations  3.81 us (1%)
    ppermute x5, waiting for transfers between devices, passed_along(): return lax.ppermute(block, axis, route)  185 us
    all_to_all x1, waiting for transfers between devices, per_device(): lax.all_to_all(jnp.stack(jnp.split(queries, lax.axis_size('uly'), axis=1)...  31.7 us
    all_to_all x1, blocking collectives, per_device(): lax.all_to_all(outputs, 'uly', split_axis=0, concat_axis=1, tiled=True)  15.9 us
    dot_general x5, matrix products, update(): jnp.einsum('qhk,khd->qhd', weights.astype(jnp.bfloat16), value_heads, pre...  14.3 us
    all_to_all x1, waiting for transfers between devices, per_device(): lax.all_to_all(values, 'uly', split_axis=1, concat_axis=0, tiled=True)  12.8 us
    another operation x10, local copies, waits for them, and re-layouts  12.6 us
    all_to_all x1, waiting for transfers between devices, per_device(): lax.all_to_all(keys, 'uly', split_axis=1, concat_axis=0, tiled=True)  10.9 us
    ppermute x5, starting transfers between devices, passed_along(): return lax.ppermute(block, axis, route)  9.37 us
  transfers between devices with their start and end apart: 8, of which 7 were waited for; matrix products, arithmetic and copies ran while one was open for 16% of the time, Pallas kernels for 0%

profile of v1, /device:TPU:8, one launch (start us, length us, event | category | flops | bytes accessed | tf_op | source)
XLA Modules:
  0.0 353.9 jit_solution(2473006433441750856)
XLA Ops:
  0.0 2.4 copy.124
  2.4 3.6 %all-to-all-start = ((bf16[128,4,768]{0,2,1:T(8,128)(2,1)}), bf16[128,4,768]{0,2,1:T(8,128)(2,1)S(1)}, u32[]{:S(2)}, u32[]{:S(2)}) async-start(bf16[128,4,768]{0,2,1:T(8,128)(2,1)} %bitcast.25), calls=%async_computation | async-start | bytes 1572864 | tf_op jit(solution)/shard_map/all_to_all | solution.py:30
  5.9 2.3 copy.126
  8.2 10.9 %all-to-all-done = bf16[128,4,768]{0,2,1:T(8,128)(2,1)S(1)} async-done(((bf16[128,4,768]{0,2,1:T(8,128)(2,1)}), bf16[128,4,768]{0,2,1:T(8,128)(2,1)S(1)}, u32[]{:S(2)}, u32[]{:S(2)}) %all-to-all-start) | async-done | bytes 786464 | tf_op jit(solution)/shard_map/all_to_all | solution.py:30
  19.1 3.6 %all-to-all-start.1 = ((bf16[128,4,768]{0,2,1:T(8,128)(2,1)}), bf16[128,4,768]{0,2,1:T(8,128)(2,1)S(1)}, u32[]{:S(2)}, u32[]{:S(2)}) async-start(bf16[128,4,768]{0,2,1:T(8,128)(2,1)} %bitcast.28), calls=%async_computation.1 | async-start | bytes 1572864 | tf_op jit(solution)/shard_map/all_to_all | solution.py:31
  23.0 12.8 %all-to-all-done.1 = bf16[128,4,768]{0,2,1:T(8,128)(2,1)S(1)} async-done(((bf16[128,4,768]{0,2,1:T(8,128)(2,1)}), bf16[128,4,768]{0,2,1:T(8,128)(2,1)S(1)}, u32[]{:S(2)}, u32[]{:S(2)}) %all-to-all-start.1) | async-done | bytes 786464 | tf_op jit(solution)/shard_map/all_to_all | solution.py:31
  36.3 9.4 %collective-permute-start = (bf16[2,512,768]{2,1,0:T(8,128)(2,1)S(1)}, bf16[2,512,768]{2,1,0:T(8,128)(2,1)S(1)}, u32[]{:S(2)}, u32[]{:S(2)}) collective-permute-start(bf16[2,512,768]{2,1,0:T(8,128)(2,1)S(1)} %pad_maximum_fusion), channel_id=1, source_target_pairs={{8,0},{12,4},{16,8},{20,12},{24,16},{28,20},{32,24},{36,28},{40,32... | collective-permute-start | bytes 4718600 | tf_op jit(solution)/shard_map/ppermute | solution.py:15
  45.7 67.2 %collective-permute-done = bf16[2,512,768]{2,1,0:T(8,128)(2,1)S(1)} collective-permute-done((bf16[2,512,768]{2,1,0:T(8,128)(2,1)S(1)}, bf16[2,512,768]{2,1,0:T(8,128)(2,1)S(1)}, u32[]{:S(2)}, u32[]{:S(2)}) %collective-permute-start) | collective-permute-done | bytes 1572896 | tf_op jit(solution)/shard_map/ppermute | solution.py:15
  112.8 40.0 %collective-permute-done.1 = bf16[2,512,768]{2,1,0:T(8,128)(2,1)S(1)} collective-permute-done((bf16[2,512,768]{2,1,0:T(8,128)(2,1)S(1)}, bf16[2,512,768]{2,1,0:T(8,128)(2,1)S(1)}, u32[]{:S(2)}, u32[]{:S(2)}) %collective-permute-start.1) | collective-permute-done | bytes 1572896 | tf_op jit(solution)/shard_map/ppermute | solution.py:15
  152.9 39.1 %collective-permute-done.2 = bf16[2,512,768]{2,1,0:T(8,128)(2,1)S(1)} collective-permute-done((bf16[2,512,768]{2,1,0:T(8,128)(2,1)S(1)}, bf16[2,512,768]{2,1,0:T(8,128)(2,1)S(1)}, u32[]{:S(2)}, u32[]{:S(2)}) %collective-permute-start.2) | collective-permute-done | bytes 1572896 | tf_op jit(solution)/shard_map/ppermute | solution.py:15
  192.0 1.2 copy-done
  193.2 38.2 %collective-permute-done.3 = bf16[2,512,768]{2,1,0:T(8,128)(2,1)} collective-permute-done((bf16[2,512,768]{2,1,0:T(8,128)(2,1)S(1)}, bf16[2,512,768]{2,1,0:T(8,128)(2,1)}, u32[]{:S(2)}, u32[]{:S(2)}) %collective-permute-start.3) | collective-permute-done | bytes 1572896 | tf_op jit(solution)/shard_map/ppermute | solution.py:15
  231.4 1.0 pad_maximum_fusion.1
  232.4 3.5 all-to-all-start.2
  236.2 0.9 compare_reduce_fusion
  237.9 0.9 compare_reduce_fusion.1
  239.5 0.9 compare_reduce_fusion.2
  241.1 0.9 compare_reduce_fusion.3
  242.7 0.9 compare_reduce_fusion.4
  244.2 31.7 %all-to-all-done.2 = bf16[4,128,768]{2,1,0:T(8,128)(2,1)S(1)} async-done(((bf16[4,128,768]{2,1,0:T(8,128)(2,1)}), bf16[4,128,768]{2,1,0:T(8,128)(2,1)S(1)}, u32[]{:S(2)}, u32[]{:S(2)}) %all-to-all-start.2) | async-done | bytes 786464 | tf_op jit(solution)/shard_map/all_to_all | solution.py:25
  276.8 10.7 %conditional.5 = (f32[512,6]{0,1:T(8,128)}, f32[512,6]{0,1:T(8,128)S(1)}, f32[512,6,128]{2,0,1:T(8,128)S(1)}) conditional(s32[]{:T(128)} %convert_element_type.67, () %tuple.38, (f32[4,4]{1,0:T(4,128)S(1)}, bf16[2,512,768]{2,1,0:T(8,128)(2,1)}, bf16[512,6,128]{0,2,1:T(8,128)(2,1)S(1)}) %tuple.118), branch_computations={%region_5.6_spmd, %region_6.0_spmd} | conditional | flops 826159104 | bytes 30290168 | solution.py:95
  277.6 1.7 copy.130
  279.4 1.3 fusion
  280.7 0.6 exponential_multiply_fusion
  281.3 2.2 fusion.2
  283.6 0.7 fusion.11
  284.3 3.2 bitcast_add_fusion
  287.5 12.0 %conditional.6 = ((f32[512,6]{0,1:T(8,128)}, f32[512,6]{0,1:T(8,128)S(1)}, f32[512,6,128]{2,0,1:T(8,128)S(1)})) conditional(s32[]{:T(128)} %convert_element_type.65, (f32[512,6]{0,1:T(8,128)}, f32[512,6]{0,1:T(8,128)S(1)}, f32[512,6,128]{2,0,1:T(8,128)S(1)}) %conditional.5, (f32[4,4]{1,0:T(4,128)S(1)}, bf16[2,512,768]{2,1,0:T(8,128)(2,1)}, ...), branch_computations={%region_9.10_spmd, %region_10.0_spmd} | conditional | flops 826546176 | bytes 31924480 | solution.py:95
  287.8 2.6 copy.133
  290.4 1.5 fusion.72
  291.9 1.3 fusion.12
  293.2 0.7 max.19
  293.9 1.5 fusion.14
  295.5 0.7 multiply_add_fusion
  296.2 2.8 bitcast_add_fusion.1
  299.0 0.6 copy.191
  299.6 12.2 %conditional.7 = ((f32[512,6]{0,1:T(8,128)}, f32[512,6]{0,1:T(8,128)S(1)}, f32[512,6,128]{2,0,1:T(8,128)S(1)})) conditional(s32[]{:T(128)} %convert_element_type.63, (f32[512,6]{0,1:T(8,128)}, f32[512,6]{0,1:T(8,128)S(1)}, f32[512,6,128]{2,0,1:T(8,128)S(1)}) %get-tuple-element.349, (f32[4,4]{1,0:T(4,128)S(1)}, bf16[2,512,768]{2,1,0:T(8,128)(2,1)}, ...), branch_computations={%region_13.14_spmd, %region_14.17_spmd} | conditional | flops 826546176 | bytes 31924480 | solution.py:95
  300.0 2.6 copy.136
  302.6 1.5 fusion.73
  304.1 1.3 fusion.23
  305.4 0.7 max.20
  306.1 1.5 fusion.25
  307.7 0.7 multiply_add_fusion.1
  308.4 2.8 bitcast_add_fusion.2
  311.2 0.6 copy.197
  311.8 12.1 %conditional.8 = ((f32[512,6]{0,1:T(8,128)}, f32[512,6]{0,1:T(8,128)S(1)}, f32[512,6,128]{2,0,1:T(8,128)S(1)})) conditional(s32[]{:T(128)} %convert_element_type.61, (f32[512,6]{0,1:T(8,128)}, f32[512,6]{0,1:T(8,128)S(1)}, f32[512,6,128]{2,0,1:T(8,128)S(1)}) %get-tuple-element.350, (f32[4,4]{1,0:T(4,128)S(1)}, bf16[2,512,768]{2,1,0:T(8,128)(2,1)}, ...), branch_computations={%region_17.18_spmd, %region_18.21_spmd} | conditional | flops 826546176 | bytes 31924480 | solution.py:95
  312.1 2.6 copy.139
  314.7 1.5 fusion.74
  316.1 1.3 fusion.34
  317.5 0.7 max.21
  318.2 1.5 fusion.36
  319.7 0.7 multiply_add_fusion.2
  320.4 2.8 bitcast_add_fusion.3
  323.2 0.6 copy.203
  323.8 11.6 %conditional.9 = ((f32[512,6]{0,1:T(8,128)S(1)}, f32[512,6,128]{2,0,1:T(8,128)S(1)})) conditional(s32[]{:T(128)} %convert_element_type.59, (f32[512,6]{0,1:T(8,128)S(1)}, f32[512,6,128]{2,0,1:T(8,128)S(1)}) %tuple.43, (f32[4,4]{1,0:T(4,128)S(1)}, bf16[2,512,768]{2,1,0:T(8,128)(2,1)}, bf16[512,6,128]{0,2,1:T(8,128)(2,1)S(1)}, f32[512,6]{0,1:T(8,128)}, ...), branch_computations={%region_21.22_spmd, %region_22.25_spmd} | conditional | flops 826546176 | bytes 31899896 | solution.py:95
  324.3 2.6 copy.142
  326.9 1.5 fusion.75
  328.4 1.3 fusion.45
  329.7 0.7 max.22
  330.4 1.5 fusion.47
  332.0 0.7 multiply_add_fusion.3
  332.7 2.8 bitcast_add_fusion.4
  336.5 15.9 %all_to_all.56 = bf16[4,128,768]{1,2,0:T(8,128)(2,1)S(1)} all-to-all(bf16[4,128,768]{1,2,0:T(8,128)(2,1)S(1)} %copy.145), channel_id=1, replica_groups=mesh['blk'=64,'uly'=4] {'uly'}, dimensions={0} | all-to-all | bytes 1572864 | tf_op jit(solution)/shard_map/all_to_all | solution.py:112
  352.5 1.2 copy.146
  (54 shorter events, 4.4 us)
Async XLA Ops:
  0.0 193.1 %copy-start.3 = (bf16[128,3072]{1,0:T(8,128)(2,1)S(1)}, bf16[128,3072]{1,0:T(8,128)(2,1)}, u32[]{:S(2)}) copy-start(bf16[128,3072]{1,0:T(8,128)(2,1)} %param.15) | copy-start | bytes 2359300
  2.4 16.7 %all-to-all-start = ((bf16[128,4,768]{0,2,1:T(8,128)(2,1)}), bf16[128,4,768]{0,2,1:T(8,128)(2,1)S(1)}, u32[]{:S(2)}, u32[]{:S(2)}) async-start(bf16[128,4,768]{0,2,1:T(8,128)(2,1)} %bitcast.25), calls=%async_computation | async-start | bytes 1572864 | tf_op jit(solution)/shard_map/all_to_all | solution.py:30
  19.1 216.8 %copy-start.4 = (s32[256]{0:T(256)S(1)}, s32[256]{0:T(256)}, u32[]{:S(2)}) copy-start(s32[256]{0:T(256)} %param.18) | copy-start | bytes 3076
  19.1 216.9 %copy-start.5 = (s32[256,20]{0,1:T(8,128)S(1)}, s32[256,20]{0,1:T(8,128)}, u32[]{:S(2)}) copy-start(s32[256,20]{0,1:T(8,128)} %param.19) | copy-start | bytes 61444
  19.1 16.8 %all-to-all-start.1 = ((bf16[128,4,768]{0,2,1:T(8,128)(2,1)}), bf16[128,4,768]{0,2,1:T(8,128)(2,1)S(1)}, u32[]{:S(2)}, u32[]{:S(2)}) async-start(bf16[128,4,768]{0,2,1:T(8,128)(2,1)} %bitcast.28), calls=%async_computation.1 | async-start | bytes 1572864 | tf_op jit(solution)/shard_map/all_to_all | solution.py:31
  36.3 76.5 %collective-permute-start = (bf16[2,512,768]{2,1,0:T(8,128)(2,1)S(1)}, bf16[2,512,768]{2,1,0:T(8,128)(2,1)S(1)}, u32[]{:S(2)}, u32[]{:S(2)}) collective-permute-start(bf16[2,512,768]{2,1,0:T(8,128)(2,1)S(1)} %pad_maximum_fusion), channel_id=1, source_target_pairs={{8,0},{12,4},{16,8},{20,12},{24,16},{28,20},{32,24},{36,28},{40,32... | collective-permute-start | bytes 4718600 | tf_op jit(solution)/shard_map/ppermute | solution.py:15
  112.8 79.1 %copy-start.2 = (bf16[2,512,768]{2,1,0:T(8,128)(2,1)}, bf16[2,512,768]{2,1,0:T(8,128)(2,1)S(1)}, u32[]{:S(2)}) copy-start(bf16[2,512,768]{2,1,0:T(8,128)(2,1)S(1)} %collective-permute-done) | copy-start | bytes 4718596
  112.8 40.0 %collective-permute-start.1 = (bf16[2,512,768]{2,1,0:T(8,128)(2,1)S(1)}, bf16[2,512,768]{2,1,0:T(8,128)(2,1)S(1)}, u32[]{:S(2)}, u32[]{:S(2)}) collective-permute-start(bf16[2,512,768]{2,1,0:T(8,128)(2,1)S(1)} %collective-permute-done), channel_id=1, source_target_pairs={{252,0},{0,4},{4,8},{8,12},{12,16},{16,20},{20,24},{24,28},{28,32}... | collective-permute-start | bytes 4718600 | tf_op jit(solution)/shard_map/ppermute | solution.py:15
  152.9 39.1 %copy-start.1 = (bf16[2,512,768]{2,1,0:T(8,128)(2,1)}, bf16[2,512,768]{2,1,0:T(8,128)(2,1)S(1)}, u32[]{:S(2)}) copy-start(bf16[2,512,768]{2,1,0:T(8,128)(2,1)S(1)} %collective-permute-done.1) | copy-start | bytes 4718596
  152.9 39.1 %collective-permute-start.2 = (bf16[2,512,768]{2,1,0:T(8,128)(2,1)S(1)}, bf16[2,512,768]{2,1,0:T(8,128)(2,1)S(1)}, u32[]{:S(2)}, u32[]{:S(2)}) collective-permute-start(bf16[2,512,768]{2,1,0:T(8,128)(2,1)S(1)} %collective-permute-done.1), channel_id=1, source_target_pairs={{252,0},{0,4},{4,8},{8,12},{12,16},{16,20},{20,24},{24,28},{28,32}... | collective-permute-start | bytes 4718600 | tf_op jit(solution)/shard_map/ppermute | solution.py:15
  192.0 1.2 copy-start
  193.1 38.3 %collective-permute-start.3 = (bf16[2,512,768]{2,1,0:T(8,128)(2,1)S(1)}, bf16[2,512,768]{2,1,0:T(8,128)(2,1)}, u32[]{:S(2)}, u32[]{:S(2)}) collective-permute-start(bf16[2,512,768]{2,1,0:T(8,128)(2,1)S(1)} %collective-permute-done.2), channel_id=1, source_target_pairs={{252,0},{0,4},{4,8},{8,12},{12,16},{16,20},{20,24},{24,28},{28,32}... | collective-permute-start | bytes 4718600 | tf_op jit(solution)/shard_map/ppermute | solution.py:15
  231.4 92.4 %collective-permute-start.4 = (bf16[2,512,768]{2,1,0:T(8,128)(2,1)}, bf16[2,512,768]{2,1,0:T(8,128)(2,1)}, u32[]{:S(2)}, u32[]{:S(2)}) collective-permute-start(bf16[2,512,768]{2,1,0:T(8,128)(2,1)} %collective-permute-done.3), channel_id=1, source_target_pairs={{252,0},{0,4},{4,8},{8,12},{12,16},{16,20},{20,24},{24,28},{28,32}... | collective-permute-start | bytes 4718600 | tf_op jit(solution)/shard_map/ppermute | solution.py:15
  232.4 43.5 %all-to-all-start.2 = ((bf16[4,128,768]{2,1,0:T(8,128)(2,1)}), bf16[4,128,768]{2,1,0:T(8,128)(2,1)S(1)}, u32[]{:S(2)}, u32[]{:S(2)}) async-start(bf16[4,128,768]{2,1,0:T(8,128)(2,1)} %pad_maximum_fusion.1), calls=%async_computation.2 | async-start | bytes 1572864 | tf_op jit(solution)/shard_map/all_to_all | solution.py:25
